TPU v7x, 32 devices: a whole 2x2x4 slice. The times are simulated.
32 devices in a mesh: layer: 8 (over z, y), feat: 4 (over x, core).
Axes of the slice: x: 2, y: 2, z: 4, core: 2. Of those that a mesh axis runs over, the one named last changes fastest.
Arguments:
- sources: bfloat16 [32, 8192], P(('layer', 'feat')), may hold values from -6 to 6
- targets: bfloat16 [32, 16384], P(('layer', 'feat')), may hold values from -16 to 16
- enc_weight: bfloat16 [8192, 32768], P(None, ('feat', 'layer')), may hold values from -0.0625 to 0.0625
- enc_bias: float32 [32768], P(('feat', 'layer')), may hold values from -3 to 3
- dec_weight: bfloat16 [32768, 16384], P('feat', 'layer'), may hold values from -0.03125 to 0.03125
- dec_bias: float32 [16384], P('layer'), may hold values from -3 to 3
Outputs:
- enc_grad: bfloat16 [8192, 32768], P(None, ('feat', 'layer'))
- dec_grad: bfloat16 [32768, 16384], P('feat', 'layer')
- mse: float32 [], replicated
All inputs are finite; a program needn't handle non-finite values.
Results may differ from a plain program's by a relative error of at most 0.011.
Values may be sent and summed in bfloat16 or wider, within the bound.
A program may use at most 192 MiB of HBM per device.

v0:
```python
import math

import jax
import jax.numpy as jnp
from jax import lax
from jax.sharding import PartitionSpec as P


def per_device(sources, targets, enc_weight, enc_bias, dec_weight, dec_bias):
    inputs = lax.all_gather(sources, ("layer", "feat"), axis=0, tiled=True)
    tokens = inputs.shape[0]
    preact = jnp.dot(inputs, enc_weight, preferred_element_type=jnp.float32) + enc_bias
    feats = jax.nn.gelu(preact).astype(jnp.bfloat16)
    n_layer = lax.axis_size("layer")
    width = dec_weight.shape[1]
    spread = lax.all_gather(targets, "feat", axis=0, tiled=True)
    blocks = spread.reshape(spread.shape[0], n_layer, width)
    owned = lax.all_to_all(blocks, "layer", split_axis=1, concat_axis=0, tiled=True)
    wanted = owned.reshape(tokens, width)
    all_feats = lax.all_gather(feats, "layer", axis=1, tiled=True)
    partial_value = jnp.dot(all_feats, dec_weight, preferred_element_type=jnp.float32)
    factor = 1.0 / math.sqrt(tokens)
    share = lax.psum_scatter(
        partial_value.astype(jnp.bfloat16), "feat", scatter_dimension=1, tiled=True
    ).astype(jnp.float32)
    columns = share.shape[1]
    first = lax.axis_index("feat") * columns
    outputs = share + lax.dynamic_slice_in_dim(dec_bias, first, columns, 0)
    misfit = outputs - lax.dynamic_slice_in_dim(wanted, first, columns, 1).astype(jnp.float32)
    errors = lax.all_gather((misfit * factor).astype(jnp.bfloat16), "feat", axis=1, tiled=True)
    total_sq = lax.psum(jnp.sum(misfit * misfit), ("layer", "feat"))
    mse = total_sq / (tokens * n_layer * width)
    dec_grad = lax.dot_general(
        all_feats, errors, (((0,), (0,)), ((), ())), preferred_element_type=jnp.float32
    ).astype(jnp.bfloat16)
    grad_rows = lax.psum_scatter(
        lax.dot_general(
            dec_weight, errors, (((1,), (1,)), ((), ())), preferred_element_type=jnp.float32
        ),
        "layer",
        scatter_dimension=0,
        tiled=True,
    )
    feat_grad = grad_rows.T
    _, pullback = jax.vjp(jax.nn.gelu, preact)
    pre_grad = pullback(feat_grad)[0].astype(jnp.bfloat16)
    enc_grad = lax.dot_general(
        inputs, pre_grad, (((0,), (0,)), ((), ())), preferred_element_type=jnp.float32
    ).astype(jnp.bfloat16)
    return (enc_grad, dec_grad, mse)


def solution(mesh):
    return jax.shard_map(
        per_device,
        mesh=mesh,
        in_specs=(
            P(("layer", "feat"), None),
            P(("layer", "feat"), None),
            P(None, ("feat", "layer")),
            P(("feat", "layer")),
            P("feat", "layer"),
            P("layer"),
        ),
        out_specs=(P(None, ("feat", "layer")), P("feat", "layer"), P()),
        check_vma=False,
    )
```

profile of v0, /device:TPU:0, one launch (start us, length us, event | category | flops | bytes accessed | tf_op | source)
XLA Modules:
  0.0 249.9 jit_solution(13598702617357543215)
XLA Ops:
  7.2 0.0 reduce-scatter.3.cloned.1.call-start
  7.2 46.4 %all-gather = bf16[32,1,8192]{2,1,0:T(2,128)(2,1)S(1)} all-gather(bf16[1,1,8192]{2,1,0:T(2,128)(2,1)} %bitcast.42), channel_id=1, replica_groups=mesh['layer'=8,'feat'=4] {'layer','feat'}, dimensions={0}, use_global_device_ids=true | all-gather | bytes 540672 | tf_op jit(solution)/shard_map/all_gather | solution.py:10
  53.6 0.0 copy-start
  53.6 8.8 %multiply_convert_fusion = (bf16[32,1024]{1,0:T(8,128)(2,1)S(1)}, f32[32,1024]{1,0:T(8,128)S(1)}) fusion(f32[1024]{0:T(1024)} %param.9, bf16[8192,1024]{1,0:T(8,128)(2,1)} %param.8, bf16[32,1,8192]{2,1,0:T(2,128)(2,1)S(1)} %all-gather), kind=kOutput, calls=%fused_computation.23 | convolution fusion | flops 537198592 | bytes 17502208 | tf_op jit(solution)/shard_map/dot_general | solution.py:12
  62.5 31.3 %all_gather.13 = bf16[32,8192]{1,0:T(8,128)(2,1)S(1)} all-gather(bf16[32,1024]{1,0:T(8,128)(2,1)S(1)} %get-tuple-element.14), channel_id=1, replica_groups=mesh['layer'=8,'feat'=4] {'layer'}, dimensions={1}, use_global_device_ids=true | all-gather | bytes 589824 | tf_op jit(solution)/shard_map/all_gather | solution.py:20
  93.8 14.2 %convolution_convert_fusion.1 = bf16[32,2048]{1,0:T(8,128)(2,1)} fusion(bf16[32,8192]{1,0:T(8,128)(2,1)S(1)} %all_gather.13, bf16[8192,2048]{1,0:T(8,128)(2,1)} %param.10), kind=kOutput, calls=%fused_computation.3 | convolution fusion | flops 1073807360 | bytes 34209792 | tf_op jit(solution)/shard_map/dot_general | solution.py:21
  108.0 0.0 reduce-scatter.3.cloned.1.call-update
  108.0 0.0 copy-done
  108.0 5.8 %all-gather.1 = bf16[4,1,16384]{2,1,0:T(2,128)(2,1)S(1)} all-gather(bf16[1,1,16384]{2,1,0:T(2,128)(2,1)S(1)} %bitcast.41), channel_id=1, replica_groups=mesh['layer'=8,'feat'=4] {'feat'}, dimensions={0}, use_global_device_ids=true | all-gather | bytes 163840 | tf_op jit(solution)/shard_map/all_gather | solution.py:16
  113.8 1.5 reduce
  115.2 3.4 %all-to-all-start = ((bf16[4,8,2048]{2,0,1:T(4,128)(2,1)}), bf16[4,8,2048]{2,0,1:T(4,128)(2,1)S(1)}, u32[]{:S(2)}, u32[]{:S(2)}) async-start(bf16[4,8,2048]{2,0,1:T(4,128)(2,1)} %bitcast.9), calls=%async_computation.1 | async-start | bytes 262144 | tf_op jit(solution)/shard_map/all_to_all | solution.py:18
  118.6 0.0 reduce-scatter.5.cloned.1.call-start
  118.7 0.8 dynamic_slice.6
  119.4 6.9 %all-to-all-done = bf16[4,8,2048]{2,0,1:T(4,128)(2,1)S(1)} async-done(((bf16[4,8,2048]{2,0,1:T(4,128)(2,1)}), bf16[4,8,2048]{2,0,1:T(4,128)(2,1)S(1)}, u32[]{:S(2)}, u32[]{:S(2)}) %all-to-all-start) | async-done | bytes 131104 | tf_op jit(solution)/shard_map/all_to_all | solution.py:18
  126.4 0.0 reduce-scatter.3.cloned.1.call-done
  126.4 1.4 multiply_reduce_fusion
  127.8 5.4 %all_gather.15 = bf16[32,2048]{1,0:T(8,128)(2,1)S(1)} all-gather(bf16[32,512]{1,0:T(8,128)(2,1)S(1)} %get-tuple-element.13), channel_id=1, replica_groups=mesh['layer'=8,'feat'=4] {'feat'}, dimensions={1}, use_global_device_ids=true | all-gather | bytes 163840 | tf_op jit(solution)/shard_map/all_gather | solution.py:30
  133.2 15.6 %convolution_bitcast_fusion = f32[8192,32]{0,1:T(8,128)} fusion(bf16[32,2048]{1,0:T(8,128)(2,1)S(1)} %all_gather.15, bf16[8192,2048]{1,0:T(8,128)(2,1)} %param.10), kind=kOutput, calls=%fused_computation.2 | convolution fusion | flops 1073741824 | bytes 34734080 | tf_op jit(solution)/shard_map/dot_general | solution.py:37
  148.8 0.0 reduce-scatter.5.cloned.1.call-update
  148.8 38.2 %psum.7 = f32[]{:T(128)} all-reduce(f32[]{:T(128)} %get-tuple-element.12), channel_id=1, replica_groups=mesh['layer'=8,'feat'=4] {'layer','feat'}, use_global_device_ids=true, to_apply=%region_3.0 | all-reduce | flops 1 | bytes 8 | tf_op jit(solution)/shard_map/psum | solution.py:31
  187.6 14.3 %convolution_convert_fusion = bf16[8192,2048]{1,0:T(8,128)(2,1)} fusion(bf16[32,8192]{1,0:T(8,128)(2,1)S(1)} %all_gather.13, bf16[32,2048]{1,0:T(8,128)(2,1)S(1)} %all_gather.15), kind=kOutput, calls=%fused_computation | convolution fusion | flops 1090519040 | bytes 34209792 | tf_op jit(solution)/shard_map/dot_general | solution.py:33
  201.9 8.6 %reduce-scatter.5.cloned.1.call-done = f32[1024,32]{0,1:T(8,128)} async-done(((f32[8192,32]{0,1:T(8,128)}), f32[1024,32]{0,1:T(8,128)}) %reduce-scatter.5.cloned.1.call-update) | async-done | bytes 131088 | tf_op jit(solution)/shard_map/reduce_scatter | solution.py:36
  210.5 9.0 %convert_bitcast_fusion = bf16[8192,1024]{0,1:T(8,128)(2,1)} fusion(bf16[32,1,8192]{2,1,0:T(2,128)(2,1)S(1)} %all-gather, f32[32,1024]{1,0:T(8,128)S(1)} %get-tuple-element.15, f32[1024,32]{0,1:T(8,128)} %reduce-scatter.5.cloned.1.call-done), kind=kOutput, calls=%fused_computation.1 | convolution fusion | flops 545914880 | bytes 17563648 | tf_op jit(solution)/shard_map/dot_general | solution.py:47
  219.5 22.4 %copy.13 = bf16[8192,1024]{1,0:T(8,128)(2,1)} copy(bf16[8192,1024]{0,1:T(8,128)(2,1)} %convert_bitcast_fusion) | data formatting | bytes 33554432
  (1 shorter events, 0.0 us)
Async XLA Ops:
  7.2 119.2 %reduce-scatter.3.cloned.1.call-start = ((), (), s32[]{:S(2)}) async-start(), calls=%async_computation.3 | async-start | bytes 163840 | tf_op jit(solution)/shard_map/reduce_scatter | solution.py:23
  53.6 54.3 %copy-start = (bf16[1,16384]{1,0:T(2,128)(2,1)S(1)}, bf16[1,16384]{1,0:T(2,128)(2,1)}, u32[]{:S(2)}) copy-start(bf16[1,16384]{1,0:T(2,128)(2,1)} %param.7) | copy-start | bytes 98308
  115.2 11.1 %all-to-all-start = ((bf16[4,8,2048]{2,0,1:T(4,128)(2,1)}), bf16[4,8,2048]{2,0,1:T(4,128)(2,1)S(1)}, u32[]{:S(2)}, u32[]{:S(2)}) async-start(bf16[4,8,2048]{2,0,1:T(4,128)(2,1)} %bitcast.9), calls=%async_computation.1 | async-start | bytes 262144 | tf_op jit(solution)/shard_map/all_to_all | solution.py:18
  118.6 91.9 %reduce-scatter.5.cloned.1.call-start = ((), (), s32[]{:S(2)}) async-start(), calls=%async_computation.4 | async-start | bytes 1179648 | tf_op jit(solution)/shard_map/reduce_scatter | solution.py:36
Sparse Core Ops, SparseCore 0:
  108.1 15.9 reduce-scatter.2
  148.9 61.5 reduce-scatter.4
where the time goes:
time: 251 us; the launch traced here: 250 us
  blocking collectives  127 us (51%)
  matrix products  61.9 us (25%)
  local copies, waits for them, and re-layouts  23.2 us (9%)
  between operations  15.9 us (6%)
  waiting for transfers between devices  15.5 us (6%)
  starting transfers between devices  3.45 us (1%)
  other arithmetic  2.86 us (1%)
    all_gather x1, blocking collectives, per_device(): inputs = lax.all_gather(sources, ('layer', 'feat'), axis=0, tiled=True)  46.4 us
    psum x1, blocking collectives, per_device(): total_sq = lax.psum(jnp.sum(misfit * misfit), ('layer', 'feat'))  38.2 us
    all_gather x1, blocking collectives, per_device(): all_feats = lax.all_gather(feats, 'layer', axis=1, tiled=True)  31.3 us
    unnamed x3, local copies, waits for them, and re-layouts  22.4 us
    dot_general x1, matrix products, per_device(): lax.dot_general(dec_weight, errors, (((1,), (1,)), ((), ())), preferred_e...  15.6 us
    dot_general x1, matrix products, per_device(): lax.dot_general(all_feats, errors, (((0,), (0,)), ((), ())), preferred_el...  14.3 us
    dot_general x1, matrix products, per_device(): jnp.dot(all_feats, dec_weight, preferred_element_type=jnp.float32)  14.2 us
    dot_general x1, matrix products, per_device(): lax.dot_general(inputs, pre_grad, (((0,), (0,)), ((), ())), preferred_ele...  9.01 us
  transfers between devices with their start and end apart: 3, of which 2 were waited for; matrix products, arithmetic and copies ran while one was open for 7% of the time, Pallas kernels for 0%

commit v1 on v0

v1 whole, which is shorter than its diff:
```python
import functools
import math

import jax
import jax.numpy as jnp
from jax import lax
from jax.experimental import pallas as pl
from jax.experimental.pallas import tpu as pltpu
from jax.sharding import PartitionSpec as P

MESH = pl.DeviceIdType.MESH
BF16 = jnp.bfloat16
F32 = jnp.float32
LANES = 128


def split2(n):
    return (n // 2, 2) if n % 2 == 0 else (n, 1)


def gather_kernel(
    nl, nf, scale, mse_scale,
    src_ref, tgt_ref, ebias_ref, dbias_ref, ew_hbm, dw_hbm,
    x_out, feats_out, err_out, pre_out, mse_out,
    ew, dw, rows, rows32, tgts, tgt32, preact, part, rs_send, rs_recv, err,
    g_send1, g_recv1, g_send2, g_recv2, sq_send, sq_recv, tot_send, tot_recv,
    ew_sem, dw_sem,
    s1_send, s1_recv, s2_send, s2_recv, s3_send, s3_recv, t_send, t_recv,
    fa_send, fa_recv, fb_send, fb_recv, rs_ssem, rs_rsem, er_send, er_recv,
    q1_send, q1_recv, q2_send, q2_recv, sq_ssem, sq_rsem, tt_ssem, tt_rsem,
):
    lo_n, li_n = split2(nl)
    fo_n, fi_n = split2(nf)
    l = lax.axis_index("layer")
    f = lax.axis_index("feat")
    lo, li = l // li_n, l % li_n
    fo, fi = f // fi_n, f % fi_n
    nk, tokens, kw = x_out.shape
    fl = feats_out.shape[2]
    tf = tokens // nf
    width = dw.shape[1]

    for k in range(nk):
        pltpu.make_async_copy(ew_hbm.at[pl.ds(k * kw, kw)], ew.at[pl.ds(k * kw, kw)], ew_sem.at[k]).start()

    def dw_copy(c):
        sl = pl.ds(pl.multiple_of(c * fl, fl), fl)
        return pltpu.make_async_copy(dw_hbm.at[sl], dw.at[sl], dw_sem.at[c])

    barrier = pltpu.get_barrier_semaphore()
    for d in range(1, nl):
        pl.semaphore_signal(barrier, inc=1, device_id=((l + d) % nl, f), device_id_type=MESH)
    for d in range(1, nf):
        pl.semaphore_signal(barrier, inc=1, device_id=(l, (f + d) % nf), device_id_type=MESH)
    pl.semaphore_wait(barrier, nl - 1 + nf - 1)

    def remote(src, dst, ssem, rsem, dev):
        return pltpu.make_async_remote_copy(
            src_ref=src, dst_ref=dst, send_sem=ssem, recv_sem=rsem, device_id=dev, device_id_type=MESH
        )

    sends = []

    def send(src, dst, ssem, rsem, dev):
        c = remote(src, dst, ssem, rsem, dev)
        c.start()
        sends.append(c)

    rows[f, l] = src_ref[...]
    for d in range(1, nl):
        to = (l + d) % nl
        send(rows.at[f, l], rows.at[f, l], s1_send.at[d], s1_recv.at[d], (to, f))
    for d in range(1, nl):
        to = (l + d) % nl
        send(tgt_ref.at[to], tgts.at[l], t_send.at[d], t_recv.at[d], (to, f))
    for c in range(nl):
        dw_copy(c).start()
    for d in range(1, nl):
        frm = (l - d + nl) % nl
        remote(rows.at[f, frm], rows.at[f, frm], s1_send.at[d], s1_recv.at[d], (frm, f)).wait_recv()
    for d in range(1, fo_n):
        to = ((fo + d) % fo_n) * fi_n + fi
        send(rows.at[f], rows.at[f], s2_send.at[d], s2_recv.at[d], (l, to))
    if fi_n == 2:
        peer = fo * fi_n + 1 - fi
        send(rows.at[f], rows.at[f], s3_send.at[0], s3_recv.at[0], (l, peer))
    for d in range(1, fo_n):
        b = ((fo - d + fo_n) % fo_n) * fi_n + fi
        remote(rows.at[b], rows.at[b], s2_send.at[d], s2_recv.at[d], (l, b)).wait_recv()
        if fi_n == 2:
            send(rows.at[b], rows.at[b], s3_send.at[d], s3_recv.at[d], (l, peer))
    if fi_n == 2:
        for d in range(fo_n):
            b = ((fo - d + fo_n) % fo_n) * fi_n + 1 - fi
            remote(rows.at[b], rows.at[b], s3_send.at[d], s3_recv.at[d], (l, peer)).wait_recv()
    per = nk * kw // LANES
    rows32[...] = rows[...].astype(F32).reshape(tokens * per, LANES)
    for s in range(per):
        at = s * LANES
        x_out[at // kw, :, at % kw : at % kw + LANES] = rows32[pl.ds(s, tokens, stride=per), :].astype(BF16)

    preact[...] = jnp.broadcast_to(ebias_ref[...], preact.shape)

    def enc_step(k, _):
        sl = pl.ds(pl.multiple_of(k * kw, kw), kw)
        pltpu.make_async_copy(ew_hbm.at[sl], ew.at[sl], ew_sem.at[k]).wait()
        preact[...] += jnp.dot(x_out[k], ew[sl, :], preferred_element_type=F32)
        return 0

    lax.fori_loop(0, nk, enc_step, 0)
    feats_out[l] = jax.nn.gelu(preact[...]).astype(BF16)

    for d in range(1, lo_n):
        to = ((lo + d) % lo_n) * li_n + li
        send(feats_out.at[l], feats_out.at[l], fa_send.at[d], fa_recv.at[d], (to, f))
    lpeer = lo * li_n + 1 - li
    if li_n == 2:
        send(feats_out.at[l], feats_out.at[l], fb_send.at[0], fb_recv.at[0], (lpeer, f))
    part[...] = jnp.zeros_like(part)

    def decode(c):
        dw_copy(c).wait()
        sl = pl.ds(pl.multiple_of(c * fl, fl), fl)
        part[...] += jnp.dot(feats_out[c], dw[sl, :], preferred_element_type=F32)

    def dec_step(d, _):
        b = ((lo - d + lo_n) % lo_n) * li_n + li

        @pl.when(d > 0)
        def _():
            remote(feats_out.at[b], feats_out.at[b], fa_send.at[d], fa_recv.at[d], (b, f)).wait_recv()
            if li_n == 2:
                remote(feats_out.at[b], feats_out.at[b], fb_send.at[d], fb_recv.at[d], (lpeer, f)).start()

        decode(b)
        return 0

    lax.fori_loop(0, lo_n, dec_step, 0)
    if li_n == 2:

        def dec_step2(d, _):
            b = ((lo - d + lo_n) % lo_n) * li_n + 1 - li
            remote(feats_out.at[b], feats_out.at[b], fb_send.at[d], fb_recv.at[d], (lpeer, f)).wait_recv()
            decode(b)
            return 0

        lax.fori_loop(0, lo_n, dec_step2, 0)

    tgts[l] = tgt_ref[l]
    for d in range(1, nl):
        frm = (l - d + nl) % nl
        remote(tgts.at[frm], tgts.at[frm], t_send.at[d], t_recv.at[d], (frm, f)).wait_recv()
    cper = width // LANES
    tgt32[...] = tgts[...].astype(F32).reshape(tf * cper, LANES)

    rs_send[...] = part[...].reshape(nf, tf, width).astype(BF16)
    for d in range(1, nf):
        to = (f + d) % nf
        send(rs_send.at[to], rs_recv.at[d], rs_ssem.at[d], rs_rsem.at[d], (l, to))
    own = part[pl.ds(pl.multiple_of(f * tf, tf), tf), :]
    own = own + dbias_ref[...]
    want = jnp.concatenate([tgt32[pl.ds(s, tf, stride=cper), :] for s in range(cper)], axis=1)
    for d in range(1, nf):
        remote(rs_recv.at[d], rs_recv.at[d], rs_ssem.at[d], rs_rsem.at[d], (l, f)).wait_recv()
        own = own + rs_recv[d].astype(F32)
    misfit = own - want
    err[f] = (misfit * scale).astype(BF16)
    for d in range(1, nf):
        to = (f + d) % nf
        send(err.at[f], err.at[f], er_send.at[d], er_recv.at[d], (l, to))
    sq = jnp.sum(misfit * misfit)
    sq_send[...] = jnp.full(sq_send.shape, sq, F32)
    for d in range(1, nf):
        to = (f + d) % nf
        send(sq_send, sq_recv.at[d], sq_ssem.at[d], sq_rsem.at[d], (l, to))
    for d in range(1, nf):
        frm = (f - d + nf) % nf
        remote(err.at[frm], err.at[frm], er_send.at[d], er_recv.at[d], (l, frm)).wait_recv()
    err_out[...] = err[...].astype(F32).reshape(tokens, width).astype(BF16)

    def grad(c):
        sl = pl.ds(pl.multiple_of(c * fl, fl), fl)
        return lax.dot_general(
            err_out[...], dw[sl, :], (((1,), (1,)), ((), ())), preferred_element_type=F32
        )

    if li_n == 2:

        def g_step1(d, _):
            o = (lo + d + 1) % lo_n
            g_send1[o] = grad(o * li_n + 1 - li).astype(BF16)
            remote(g_send1.at[o], g_recv1.at[o], q1_send.at[o], q1_recv.at[o], (lpeer, f)).start()
            return 0

        lax.fori_loop(0, lo_n, g_step1, 0)

    def peer_part(o):
        remote(g_recv1.at[o], g_recv1.at[o], q1_send.at[o], q1_recv.at[o], (lpeer, f)).wait_recv()
        return g_recv1[o].astype(F32)

    def g_step2(d, _):
        o = (lo + d) % lo_n
        g = grad(o * li_n + li)
        if li_n == 2:
            g = g + peer_part(o)
        g_send2[d] = g.astype(BF16)
        remote(g_send2.at[d], g_recv2.at[d], q2_send.at[d], q2_recv.at[d], (o * li_n + li, f)).start()
        return 0

    lax.fori_loop(1, lo_n, g_step2, 0)

    tot = sq_send[...]
    for d in range(1, nf):
        remote(sq_recv.at[d], sq_recv.at[d], sq_ssem.at[d], sq_rsem.at[d], (l, f)).wait_recv()
        tot = tot + sq_recv[d]
    tot_send[...] = tot
    for d in range(1, nl):
        send(tot_send, tot_recv.at[d], tt_ssem.at[d], tt_rsem.at[d], ((l + d) % nl, f))

    g = grad(l)
    if li_n == 2:
        g = g + peer_part(lo)
    _, pullback = jax.vjp(jax.nn.gelu, preact[...])
    for d in range(1, nl):
        remote(tot_recv.at[d], tot_recv.at[d], tt_ssem.at[d], tt_rsem.at[d], (l, f)).wait_recv()
        tot = tot + tot_recv[d]
    mse_out[...] = tot * mse_scale
    for d in range(1, lo_n):
        remote(g_recv2.at[d], g_recv2.at[d], q2_send.at[d], q2_recv.at[d], (l, f)).wait_recv()
        g = g + g_recv2[d].astype(F32)
    pre_out[...] = pullback(g)[0].astype(BF16)

    for c in sends:
        c.wait_send()
    for d in range(1, lo_n):
        remote(g_send2.at[d], g_recv2.at[d], q2_send.at[d], q2_recv.at[d], (l, f)).wait_send()
        if li_n == 2:
            b = ((lo - d + lo_n) % lo_n) * li_n + li
            remote(feats_out.at[b], feats_out.at[b], fb_send.at[d], fb_recv.at[d], (lpeer, f)).wait_send()
    if li_n == 2:
        for o in range(lo_n):
            remote(g_send1.at[o], g_recv1.at[o], q1_send.at[o], q1_recv.at[o], (lpeer, f)).wait_send()


def outer_kernel(n1, a1_ref, b1_ref, a2_ref, b2_ref, o1_ref, o2_ref):
    i = pl.program_id(0)
    dims = (((0,), (0,)), ((), ()))

    @pl.when(i < n1)
    def _():
        o1_ref[...] = lax.dot_general(a1_ref[0], b1_ref[...], dims, preferred_element_type=F32).astype(BF16)

    @pl.when(i >= n1)
    def _():
        o2_ref[...] = lax.dot_general(a2_ref[0], b2_ref[...], dims, preferred_element_type=F32).astype(BF16)


def per_device(sources, targets, enc_weight, enc_bias, dec_weight, dec_bias):
    nl, nf = lax.axis_size("layer"), lax.axis_size("feat")
    lo_n, _ = split2(nl)
    fo_n, _ = split2(nf)
    r, depth = sources.shape
    tokens = r * nl * nf
    fl = enc_weight.shape[1]
    block, width = dec_weight.shape
    tf = tokens // nf
    kw = 1024
    nk = depth // kw
    per, cper = depth // LANES, width // LANES
    src = sources.reshape(r * per, LANES)
    tgt = targets.reshape(r, nl, cper, LANES).transpose(1, 0, 2, 3).reshape(nl, r * cper, LANES)
    dma = pltpu.SemaphoreType.DMA
    vmem = pl.BlockSpec(memory_space=pltpu.VMEM)
    hbm = pl.BlockSpec(memory_space=pl.ANY)
    sds = jax.ShapeDtypeStruct
    x, feats, errors, pre_grad, mse = pl.pallas_call(
        functools.partial(
            gather_kernel, nl, nf, 1.0 / math.sqrt(tokens), 1.0 / (tokens * nl * width)
        ),
        out_shape=(
            sds((nk, tokens, kw), BF16),
            sds((nl, tokens, fl), BF16),
            sds((tokens, width), BF16),
            sds((tokens, fl), BF16),
            sds((8, LANES), F32),
        ),
        in_specs=[vmem, vmem, vmem, vmem, hbm, hbm],
        out_specs=(vmem,) * 5,
        scratch_shapes=[
            pltpu.VMEM((depth, fl), BF16),
            pltpu.VMEM((block, width), BF16),
            pltpu.VMEM((nf, nl, r * per, LANES), BF16),
            pltpu.VMEM((tokens * per, LANES), F32),
            pltpu.VMEM((nl, r * cper, LANES), BF16),
            pltpu.VMEM((tf * cper, LANES), F32),
            pltpu.VMEM((tokens, fl), F32),
            pltpu.VMEM((tokens, width), F32),
            pltpu.VMEM((nf, tf, width), BF16),
            pltpu.VMEM((nf, tf, width), BF16),
            pltpu.VMEM((nf, tf, width), BF16),
            pltpu.VMEM((lo_n, tokens, fl), BF16),
            pltpu.VMEM((lo_n, tokens, fl), BF16),
            pltpu.VMEM((lo_n, tokens, fl), BF16),
            pltpu.VMEM((lo_n, tokens, fl), BF16),
            pltpu.VMEM((8, LANES), F32),
            pltpu.VMEM((nf, 8, LANES), F32),
            pltpu.VMEM((8, LANES), F32),
            pltpu.VMEM((nl, 8, LANES), F32),
            dma((nk,)), dma((nl,)),
            dma((nl,)), dma((nl,)), dma((fo_n,)), dma((fo_n,)), dma((fo_n,)), dma((fo_n,)),
            dma((nl,)), dma((nl,)),
            dma((lo_n,)), dma((lo_n,)), dma((lo_n,)), dma((lo_n,)),
            dma((nf,)), dma((nf,)), dma((nf,)), dma((nf,)),
            dma((lo_n,)), dma((lo_n,)), dma((lo_n,)), dma((lo_n,)),
            dma((nf,)), dma((nf,)), dma((nl,)), dma((nl,)),
        ],
        compiler_params=pltpu.CompilerParams(
            collective_id=0, has_side_effects=True, vmem_limit_bytes=62 * 2**20
        ),
        name="gather",
    )(src, tgt, enc_bias.reshape(1, fl), dec_bias.reshape(1, width), enc_weight, dec_weight)

    rb1 = min(512, fl)
    rb2 = min(1024, kw)
    n1, n2 = block // rb1, depth // rb2
    p1, p2 = fl // rb1, kw // rb2

    def i1(i):
        return jnp.minimum(i, n1 - 1)

    def i2(i):
        return jnp.maximum(i - n1, 0)

    dec_grad, enc_grad = pl.pallas_call(
        functools.partial(outer_kernel, n1),
        grid=(n1 + n2,),
        out_shape=(sds((block, width), BF16), sds((depth, fl), BF16)),
        in_specs=[
            pl.BlockSpec((1, tokens, rb1), lambda i: (i1(i) // p1, 0, i1(i) % p1)),
            pl.BlockSpec((tokens, width), lambda i: (0, 0)),
            pl.BlockSpec((1, tokens, rb2), lambda i: (i2(i) // p2, 0, i2(i) % p2)),
            pl.BlockSpec((tokens, fl), lambda i: (0, 0)),
        ],
        out_specs=(
            pl.BlockSpec((rb1, width), lambda i: (i1(i), 0)),
            pl.BlockSpec((rb2, fl), lambda i: (i2(i), 0)),
        ),
        compiler_params=pltpu.CompilerParams(vmem_limit_bytes=48 * 2**20),
        name="outer",
    )(feats, errors, x, pre_grad)
    return (enc_grad, dec_grad, mse[0, 0])


def solution(mesh):
    return jax.shard_map(
        per_device,
        mesh=mesh,
        in_specs=(
            P(("layer", "feat"), None),
            P(("layer", "feat"), None),
            P(None, ("feat", "layer")),
            P(("feat", "layer")),
            P("feat", "layer"),
            P("layer"),
        ),
        out_specs=(P(None, ("feat", "layer")), P("feat", "layer"), P()),
        check_vma=False,
    )
```

time: 251 us -> 93.8 us (0.37)
  blocking collectives: 127 us -> 0 us
  Pallas kernels: 0 us -> 84.5 us
  matrix products: 61.9 us -> 0 us
  local copies, waits for them, and re-layouts: 23.2 us -> 5.01 us
  waiting for transfers between devices: 15.5 us -> 0 us
  between operations: 15.9 us -> 0.64 us
  starting transfers between devices: 3.45 us -> 0 us
    all_gather x4 -> x0, blocking collectives: 88.9 us -> none  [the longest x1 46.4 us: per_device(): inputs = lax.all_gather(sources, ('layer', 'feat'), axis=0, tiled=True)]
    pallas_call x0 -> x2, Pallas kernels: none -> 84.5 us  [the longest x1 58.6 us: per_device(): pl.pallas_call(functools.partial(gather_kernel, nl, nf, 1.0 / math.sqrt(t...]
    dot_general x5 -> x0, matrix products: 61.9 us -> none  [the longest x1 15.6 us: per_device(): lax.dot_general(dec_weight, errors, (((1,), (1,)), ((), ())), preferred_e...]
    psum x1 -> x0, blocking collectives: 38.2 us -> none  [per_device(): total_sq = lax.psum(jnp.sum(misfit * misfit), ('layer', 'feat'))]
    unnamed x3 -> x8, local copies, waits for them, and re-layouts: 22.4 us -> 3.82 us
    reduce_scatter x2 -> x0, waiting for transfers between devices: 8.59 us -> none  [the longest x1 8.57 us: per_device(): lax.psum_scatter(lax.dot_general(dec_weight, errors, (((1,), (1,)), ((),...]
    all_to_all x1 -> x0, waiting for transfers between devices: 6.89 us -> none  [per_device(): lax.all_to_all(blocks, 'layer', split_axis=1, concat_axis=0, tiled=True)]
    all_to_all x1 -> x0, starting transfers between devices: 3.37 us -> none  [per_device(): lax.all_to_all(blocks, 'layer', split_axis=1, concat_axis=0, tiled=True)]
  transfers between devices with their start and end apart: 3 -> 0, of which waited for: 2 -> 0; matrix products, arithmetic and copies ran while one was open for 7% -> 0% of each run, Pallas kernels for 0% -> 0%
where the time goes in v1:
time: 93.8 us; the launch traced here: 93.3 us
  Pallas kernels  84.5 us (90%)
  local copies, waits for them, and re-layouts  5.01 us (5%)
  other arithmetic  3.08 us (3%)
    pallas_call x1, Pallas kernels, per_device(): pl.pallas_call(functools.partial(gather_kernel, nl, nf, 1.0 / math.sqrt(t...  58.6 us
    pallas_call x1, Pallas kernels, per_device(): pl.pallas_call(functools.partial(outer_kernel, n1), grid=(n1 + n2,), out_...  26 us
    unnamed x8, local copies, waits for them, and re-layouts  3.82 us
    unnamed x2, other arithmetic  3.08 us

profile of v1, /device:TPU:0, one launch (start us, length us, event | category | flops | bytes accessed | tf_op | source)
XLA Modules:
  0.0 93.3 jit_solution(5737643190546740292)
XLA Ops:
  0.6 1.5 %reduce = bf16[8192]{0:T(1024)(128)(2,1)} reduce(bf16[1,8192]{1,0:T(2,128)(2,1)} %param.6, bf16[]{:T(256)} %constant.2), dimensions={0}, to_apply=%param.6.reduce_sub_computation | reduce | bytes 32770 | tf_op args[0]
  2.1 1.6 %reduce.1 = bf16[16384]{0:T(1024)(128)(2,1)} reduce(bf16[1,16384]{1,0:T(2,128)(2,1)} %param.7, bf16[]{:T(256)} %constant.2), dimensions={0}, to_apply=%param.7.reduce_sub_computation | reduce | bytes 65538 | tf_op args[1]
  3.7 58.6 %gather.1 = (bf16[8,32,1024]{2,1,0:T(8,128)(2,1)}, bf16[8,32,1024]{2,1,0:T(8,128)(2,1)}, bf16[32,2048]{1,0:T(8,128)(2,1)}, bf16[32,1024]{1,0:T(8,128)(2,1)}, f32[8,128]{1,0:T(8,128)}) custom-call(bf16[64,128]{1,0:T(8,128)(2,1)} %bitcast.6, bf16[8,16,128]{2,1,0:T(8,128)(2,1)} %bitcast.5, f32[1,1024]{1,0:T(1,128)} %bitcast.8, f32[1,2048]{1,0:T(1,128)} %bitcast.7, ...), custom_call_target="tpu_custom_call" | custom-call | tf_op jit(solution)/shard_map/gather/pallas_call | solution.py:276
  62.3 1.2 %slice.3 = f32[1,1]{1,0:T(1,128)} slice(f32[8,128]{1,0:T(8,128)} %get-tuple-element.16), slice={[0:1], [0:1]} | slice | bytes 8 | tf_op jit(solution)/shard_map/slice | solution.py:351
  63.5 0.0 copy-start
  63.5 1.0 %copy-done = bf16[8,32,1024]{2,1,0:T(8,128)(2,1)S(1)} copy-done((bf16[8,32,1024]{2,1,0:T(8,128)(2,1)S(1)}, bf16[8,32,1024]{2,1,0:T(8,128)(2,1)}, u32[]{:S(2)}) %copy-start) | copy-done | bytes 524312
  64.5 0.0 copy-start.1
  64.5 1.0 %copy-done.1 = bf16[8,32,1024]{2,1,0:T(8,128)(2,1)S(1)} copy-done((bf16[8,32,1024]{2,1,0:T(8,128)(2,1)S(1)}, bf16[8,32,1024]{2,1,0:T(8,128)(2,1)}, u32[]{:S(2)}) %copy-start.1) | copy-done | bytes 524312
  65.5 0.0 copy-start.2
  65.6 0.9 copy-done.2
  66.5 0.0 copy-start.3
  66.5 0.8 copy-done.3
  67.3 26.0 %outer.1 = (bf16[8192,2048]{1,0:T(8,128)(2,1)}, bf16[8192,1024]{1,0:T(8,128)(2,1)}) custom-call(bf16[8,32,1024]{2,1,0:T(8,128)(2,1)S(1)} %copy-done.1, bf16[32,2048]{1,0:T(8,128)(2,1)S(1)} %copy-done.2, bf16[8,32,1024]{2,1,0:T(8,128)(2,1)S(1)} %copy-done, bf16[32,1024]{1,0:T(8,128)(2,1)S(1)} %copy-done.3), custom_call_target="tpu_custom_call" | custom-call | tf_op jit(solution)/shard_map/outer/pallas_call | solution.py:334
Async XLA Ops:
  63.5 1.0 %copy-start = (bf16[8,32,1024]{2,1,0:T(8,128)(2,1)S(1)}, bf16[8,32,1024]{2,1,0:T(8,128)(2,1)}, u32[]{:S(2)}) copy-start(bf16[8,32,1024]{2,1,0:T(8,128)(2,1)} %get-tuple-element.12.a2_ref) | copy-start | bytes 1572868
  64.5 1.0 %copy-start.1 = (bf16[8,32,1024]{2,1,0:T(8,128)(2,1)S(1)}, bf16[8,32,1024]{2,1,0:T(8,128)(2,1)}, u32[]{:S(2)}) copy-start(bf16[8,32,1024]{2,1,0:T(8,128)(2,1)} %get-tuple-element.10.a1_ref) | copy-start | bytes 1572868
  65.5 0.9 copy-start.2
  66.5 0.8 copy-start.3

commit v2 on v1

--- a/solution.py
+++ b/solution.py
@@ -20,9 +20,9 @@
 
 def gather_kernel(
     nl, nf, scale, mse_scale,
-    src_ref, tgt_ref, ebias_ref, dbias_ref, ew_hbm, dw_hbm,
+    src_in, tgt_in, ebias_ref, dbias_ref, ew_hbm, dw_hbm,
     x_out, feats_out, err_out, pre_out, mse_out,
-    ew, dw, rows, rows32, tgts, tgt32, preact, part, rs_send, rs_recv, err,
+    ew, dw, rows, rows32, tgt_ref, tgt_stage, tgts, tgt32, preact, part, rs_send, rs_recv, err,
     g_send1, g_recv1, g_send2, g_recv2, sq_send, sq_recv, tot_send, tot_recv,
     ew_sem, dw_sem,
     s1_send, s1_recv, s2_send, s2_recv, s3_send, s3_recv, t_send, t_recv,
@@ -40,12 +40,29 @@
     tf = tokens // nf
     width = dw.shape[1]
 
+    per = nk * kw // LANES
+    cper = width // LANES
     for k in range(nk):
         pltpu.make_async_copy(ew_hbm.at[pl.ds(k * kw, kw)], ew.at[pl.ds(k * kw, kw)], ew_sem.at[k]).start()
 
     def dw_copy(c):
         sl = pl.ds(pl.multiple_of(c * fl, fl), fl)
         return pltpu.make_async_copy(dw_hbm.at[sl], dw.at[sl], dw_sem.at[c])
+
+    r = src_in.shape[0]
+    own_rows = src_in[...].astype(F32)
+    for i in range(r):
+        for s in range(per):
+            rows32[i * per + s : i * per + s + 1, :] = own_rows[i : i + 1, s * LANES : (s + 1) * LANES]
+    own_tgt = tgt_in[...].astype(F32)
+    for c in range(nl):
+        for i in range(r):
+            for s in range(cper):
+                col = (c * cper + s) * LANES
+                row = i * cper + s
+                tgt_stage[c, row : row + 1, :] = own_tgt[i : i + 1, col : col + LANES]
+    tgt_ref[...] = tgt_stage[...].astype(BF16)
+    rows[f, l] = rows32[: r * per, :].astype(BF16)
 
     barrier = pltpu.get_barrier_semaphore()
     for d in range(1, nl):
@@ -66,7 +83,6 @@
         c.start()
         sends.append(c)
 
-    rows[f, l] = src_ref[...]
     for d in range(1, nl):
         to = (l + d) % nl
         send(rows.at[f, l], rows.at[f, l], s1_send.at[d], s1_recv.at[d], (to, f))
@@ -93,7 +109,6 @@
         for d in range(fo_n):
             b = ((fo - d + fo_n) % fo_n) * fi_n + 1 - fi
             remote(rows.at[b], rows.at[b], s3_send.at[d], s3_recv.at[d], (l, peer)).wait_recv()
-    per = nk * kw // LANES
     rows32[...] = rows[...].astype(F32).reshape(tokens * per, LANES)
     for s in range(per):
         at = s * LANES
@@ -150,7 +165,6 @@
     for d in range(1, nl):
         frm = (l - d + nl) % nl
         remote(tgts.at[frm], tgts.at[frm], t_send.at[d], t_recv.at[d], (frm, f)).wait_recv()
-    cper = width // LANES
     tgt32[...] = tgts[...].astype(F32).reshape(tf * cper, LANES)
 
     rs_send[...] = part[...].reshape(nf, tf, width).astype(BF16)
@@ -242,17 +256,62 @@
             remote(g_send1.at[o], g_recv1.at[o], q1_send.at[o], q1_recv.at[o], (lpeer, f)).wait_send()
 
 
-def outer_kernel(n1, a1_ref, b1_ref, a2_ref, b2_ref, o1_ref, o2_ref):
-    i = pl.program_id(0)
+def outer_kernel(a1_ref, b1_ref, a2_ref, b2_ref, m_ref, o1_hbm, o2_hbm, o3_ref, o1, o2, sem1, sem2):
     dims = (((0,), (0,)), ((), ()))
-
-    @pl.when(i < n1)
-    def _():
-        o1_ref[...] = lax.dot_general(a1_ref[0], b1_ref[...], dims, preferred_element_type=F32).astype(BF16)
-
-    @pl.when(i >= n1)
-    def _():
-        o2_ref[...] = lax.dot_general(a2_ref[0], b2_ref[...], dims, preferred_element_type=F32).astype(BF16)
+    o3_ref[0, 0] = jnp.max(m_ref[...])
+
+    def copy(out, hbm, sem, j, n):
+        sl = pl.ds(pl.multiple_of(j * n, n), n)
+        return pltpu.make_async_copy(out.at[sl], hbm.at[sl], sem.at[j])
+
+    def run(left, right, out, hbm, sem):
+        count, _, n = left.shape
+
+        def step(j, _):
+            out[pl.ds(pl.multiple_of(j * n, n), n), :] = lax.dot_general(
+                left[j], right[...], dims, preferred_element_type=F32
+            ).astype(BF16)
+            copy(out, hbm, sem, j, n).start()
+            return 0
+
+        lax.fori_loop(0, count, step, 0)
+
+    def finish(left, out, hbm, sem):
+        count, _, n = left.shape
+
+        def step(j, _):
+            copy(out, hbm, sem, j, n).wait()
+            return 0
+
+        lax.fori_loop(0, count, step, 0)
+
+    run(a2_ref, b2_ref, o2, o2_hbm, sem2)
+    run(a1_ref, b1_ref, o1, o1_hbm, sem1)
+    finish(a2_ref, o2, o2_hbm, sem2)
+    finish(a1_ref, o1, o1_hbm, sem1)
+
+
+def outer(feats, errors, x, pre_grad, mse):
+    nl, tokens, fl = feats.shape
+    nk, _, kw = x.shape
+    width = errors.shape[1]
+    vmem = pl.BlockSpec(memory_space=pltpu.VMEM)
+    hbm = pl.BlockSpec(memory_space=pl.ANY)
+    sds = jax.ShapeDtypeStruct
+    return pl.pallas_call(
+        outer_kernel,
+        out_shape=(sds((nl * fl, width), BF16), sds((nk * kw, fl), BF16), sds((1, 1), F32)),
+        in_specs=[vmem] * 5,
+        out_specs=(hbm, hbm, pl.BlockSpec(memory_space=pltpu.SMEM)),
+        scratch_shapes=[
+            pltpu.VMEM((nl * fl, width), BF16),
+            pltpu.VMEM((nk * kw, fl), BF16),
+            pltpu.SemaphoreType.DMA((nl,)),
+            pltpu.SemaphoreType.DMA((nk,)),
+        ],
+        compiler_params=pltpu.CompilerParams(vmem_limit_bytes=62 * 2**20),
+        name="outer",
+    )(feats, errors, x, pre_grad, mse)
 
 
 def per_device(sources, targets, enc_weight, enc_bias, dec_weight, dec_bias):
@@ -267,8 +326,6 @@
     kw = 1024
     nk = depth // kw
     per, cper = depth // LANES, width // LANES
-    src = sources.reshape(r * per, LANES)
-    tgt = targets.reshape(r, nl, cper, LANES).transpose(1, 0, 2, 3).reshape(nl, r * cper, LANES)
     dma = pltpu.SemaphoreType.DMA
     vmem = pl.BlockSpec(memory_space=pltpu.VMEM)
     hbm = pl.BlockSpec(memory_space=pl.ANY)
@@ -291,6 +348,8 @@
             pltpu.VMEM((block, width), BF16),
             pltpu.VMEM((nf, nl, r * per, LANES), BF16),
             pltpu.VMEM((tokens * per, LANES), F32),
+            pltpu.VMEM((nl, r * cper, LANES), BF16),
+            pltpu.VMEM((nl, r * cper, LANES), F32),
             pltpu.VMEM((nl, r * cper, LANES), BF16),
             pltpu.VMEM((tf * cper, LANES), F32),
             pltpu.VMEM((tokens, fl), F32),
@@ -318,37 +377,10 @@
             collective_id=0, has_side_effects=True, vmem_limit_bytes=62 * 2**20
         ),
         name="gather",
-    )(src, tgt, enc_bias.reshape(1, fl), dec_bias.reshape(1, width), enc_weight, dec_weight)
-
-    rb1 = min(512, fl)
-    rb2 = min(1024, kw)
-    n1, n2 = block // rb1, depth // rb2
-    p1, p2 = fl // rb1, kw // rb2
-
-    def i1(i):
-        return jnp.minimum(i, n1 - 1)
-
-    def i2(i):
-        return jnp.maximum(i - n1, 0)
-
-    dec_grad, enc_grad = pl.pallas_call(
-        functools.partial(outer_kernel, n1),
-        grid=(n1 + n2,),
-        out_shape=(sds((block, width), BF16), sds((depth, fl), BF16)),
-        in_specs=[
-            pl.BlockSpec((1, tokens, rb1), lambda i: (i1(i) // p1, 0, i1(i) % p1)),
-            pl.BlockSpec((tokens, width), lambda i: (0, 0)),
-            pl.BlockSpec((1, tokens, rb2), lambda i: (i2(i) // p2, 0, i2(i) % p2)),
-            pl.BlockSpec((tokens, fl), lambda i: (0, 0)),
-        ],
-        out_specs=(
-            pl.BlockSpec((rb1, width), lambda i: (i1(i), 0)),
-            pl.BlockSpec((rb2, fl), lambda i: (i2(i), 0)),
-        ),
-        compiler_params=pltpu.CompilerParams(vmem_limit_bytes=48 * 2**20),
-        name="outer",
-    )(feats, errors, x, pre_grad)
-    return (enc_grad, dec_grad, mse[0, 0])
+    )(sources, targets, enc_bias.reshape(1, fl), dec_bias.reshape(1, width), enc_weight, dec_weight)
+
+    dec_grad, enc_grad, mean_sq = outer(feats, errors, x, pre_grad, mse)
+    return (enc_grad, dec_grad, mean_sq.reshape(()))
 
 
 def solution(mesh):

time: 93.8 us -> 79.7 us (0.85)
  Pallas kernels: 84.5 us -> 78.9 us
  local copies, waits for them, and re-layouts: 5.01 us -> 0 us
  other arithmetic: 3.08 us -> 0 us
    pallas_call x1, Pallas kernels: 26 us -> 20.2 us  [outer(): pl.pallas_call(outer_kernel, out_shape=(sds((nl * fl, width), BF16), sds(...]
    unnamed x8 -> x0, local copies, waits for them, and re-layouts: 3.82 us -> none
    unnamed x2 -> x0, other arithmetic: 3.08 us -> none
    slice x1 -> x0, local copies, waits for them, and re-layouts: 1.18 us -> none  [per_device(): return (enc_grad, dec_grad, mse[0, 0])]
where the time goes in v2:
time: 79.7 us; the launch traced here: 79.5 us
  Pallas kernels  78.9 us (99%)
    pallas_call x1, Pallas kernels, per_device(): pl.pallas_call(functools.partial(gather_kernel, nl, nf, 1.0 / math.sqrt(t...  58.7 us
    pallas_call x1, Pallas kernels, outer(): pl.pallas_call(outer_kernel, out_shape=(sds((nl * fl, width), BF16), sds(...  20.2 us

profile of v2, /device:TPU:0, one launch (start us, length us, event | category | flops | bytes accessed | tf_op | source)
XLA Modules:
  0.0 79.5 jit_solution(15140783583289566548)
XLA Ops:
  0.6 58.7 %gather.1 = (bf16[8,32,1024]{2,1,0:T(8,128)(2,1)}, bf16[8,32,1024]{2,1,0:T(8,128)(2,1)}, bf16[32,2048]{1,0:T(8,128)(2,1)}, bf16[32,1024]{1,0:T(8,128)(2,1)}, f32[8,128]{1,0:T(8,128)}) custom-call(bf16[1,8192]{1,0:T(2,128)(2,1)} %src_in.1, bf16[1,16384]{1,0:T(2,128)(2,1)} %tgt_in.1, f32[1,1024]{1,0:T(1,128)} %bitcast.4, f32[1,2048]{1,0:T(1,128)} %bitcast.3, ...), custom_call_target="tpu_custom_call" | custom-call | tf_op jit(solution)/shard_map/gather/pallas_call | solution.py:333
  59.3 20.2 %outer.1 = (bf16[8192,2048]{1,0:T(8,128)(2,1)}, bf16[8192,1024]{1,0:T(8,128)(2,1)}, f32[1,1]{1,0:T(1,128)}) custom-call(bf16[8,32,1024]{2,1,0:T(8,128)(2,1)} %get-tuple-element.11.a1_ref, bf16[32,2048]{1,0:T(8,128)(2,1)} %get-tuple-element.12.b1_ref, bf16[8,32,1024]{2,1,0:T(8,128)(2,1)} %get-tuple-element.13.a2_ref, ...), custom_call_target="tpu_custom_call" | custom-call | tf_op jit(solution)/shard_map/outer/pallas_call | solution.py:301
